TPU v7x, 128 devices: a whole 4x4x4 slice. The times are simulated.
128 devices in a mesh: row: 16 (over z, y), col: 8 (over x, core).
Axes of the slice: x: 4, y: 4, z: 4, core: 2. Of those that a mesh axis runs over, the one named last changes fastest.
Arguments:
- rhs_leaf: bfloat16 [128, 2048, 128], P(('row', 'col')), may hold values from -6 to 6
- rhs_sep: bfloat16 [2048, 128], P('col'), may hold values from -6 to 6
- leaf_sizes: int32 [128], P(('row', 'col')), may hold values from 512 to 2048, as said below
- off_blocks: int32 [128, 4], P(('row', 'col')), may hold values from 0 to 15, as said below
- linv_leaf: bfloat16 [128, 2048, 2048], P(('row', 'col')), as said below
- uinv_leaf: bfloat16 [128, 2048, 2048], P(('row', 'col')), as said below
- l_off: bfloat16 [128, 512, 2048], P(('row', 'col')), may hold values from -0.0234375 to 0.0234375
- u_off: bfloat16 [128, 2048, 512], P(('row', 'col')), may hold values from -0.25 to 0.25
- linv_sep: bfloat16 [2048, 2048], P('row', 'col'), as said below
- uinv_sep: bfloat16 [2048, 2048], P('row', 'col'), as said below
Outputs:
- solved_leaf: bfloat16 [128, 2048, 128], P(('row', 'col'))
- solved_sep: bfloat16 [2048, 128], P('row')
Inputs may be any that keep to these rules, and one draw needn't show every extreme that they name: `leaf_sizes`: between 512 and 2048; the first leaf has exactly 2048. `off_blocks`: the 4 blocks of each leaf are different. `linv_leaf`: lower triangular, diagonal between 0.5 and 1.5. `uinv_leaf`: upper triangular, diagonal between 0.5 and 1.5. `linv_sep`: lower triangular, diagonal between 0.5 and 1.5. `uinv_sep`: upper triangular, diagonal between 0.5 and 1.5.
All inputs are finite; a program needn't handle non-finite values.
Results may differ from a plain program's by a relative error of at most 0.013.
Values may be sent and summed in bfloat16 or wider, within the bound.
A program may use at most 64 MiB of HBM per device.

v0:
```python
import jax
import jax.numpy as jnp
from jax import lax
from jax.sharding import PartitionSpec as P

S = 2048
BLK = 128
KB = 4
SB = 16


def shards(
    rhs_leaf,
    rhs_sep,
    leaf_sizes,
    off_blocks,
    linv_leaf,
    uinv_leaf,
    l_off,
    u_off,
    linv_sep,
    uinv_sep,
):
    leaf_count = rhs_leaf.shape[0]
    row_count = rhs_leaf.shape[1]
    columns_rhs = rhs_leaf.shape[2]
    positions = jnp.arange(row_count, dtype=jnp.int32)
    keep_rows = (positions[None, :] < leaf_sizes[:, None])[:, :, None]
    masked = jnp.where(keep_rows, rhs_leaf, jnp.zeros_like(rhs_leaf))
    forward = jnp.einsum("lij,ljk->lik", linv_leaf, masked, preferred_element_type=jnp.float32)
    forward = jnp.where(keep_rows, forward, 0.0).astype(jnp.bfloat16)
    updates = jnp.einsum("lpj,ljk->lpk", l_off, forward, preferred_element_type=jnp.float32)
    updates = updates.reshape(leaf_count, KB, BLK * columns_rhs)
    selector = (off_blocks[:, :, None] == jnp.arange(SB, dtype=jnp.int32)[None, None, :]).astype(
        jnp.float32
    )
    partial_sum = jnp.einsum("lks,lkr->sr", selector, updates, precision=lax.Precision.HIGHEST)
    partial_sum = partial_sum.reshape(S, columns_rhs)
    share_count = rhs_sep.shape[0]
    col_start = lax.axis_index("col") * share_count
    coupled_sum = lax.psum(partial_sum, ("row", "col"))
    coupled_share = lax.dynamic_slice_in_dim(coupled_sum, col_start, share_count, 0)
    sep_rhs = (rhs_sep.astype(jnp.float32) - coupled_share).astype(jnp.bfloat16)
    forward_terms = jnp.dot(linv_sep, sep_rhs, preferred_element_type=jnp.float32)
    forward_rows = lax.psum(forward_terms, "col").astype(jnp.bfloat16)
    sep_forward = lax.all_gather(forward_rows, "row", axis=0, tiled=True)
    forward_share = lax.dynamic_slice_in_dim(sep_forward, col_start, share_count, 0)
    solved_terms = jnp.dot(uinv_sep, forward_share, preferred_element_type=jnp.float32)
    solved_rows = lax.psum(solved_terms, "col").astype(jnp.bfloat16)
    solved_sep = lax.all_gather(solved_rows, "row", axis=0, tiled=True)
    sep_blocks = solved_sep.reshape(SB, BLK, columns_rhs)
    coupled = sep_blocks[off_blocks].reshape(leaf_count, KB * BLK, columns_rhs)
    residue = forward.astype(jnp.float32) - jnp.einsum(
        "ljp,lpk->ljk", u_off, coupled, preferred_element_type=jnp.float32
    )
    residue = jnp.where(keep_rows, residue, 0.0).astype(jnp.bfloat16)
    solved = jnp.einsum("lij,ljk->lik", uinv_leaf, residue, preferred_element_type=jnp.float32)
    solved_leaf = jnp.where(keep_rows, solved, 0.0).astype(jnp.bfloat16)
    return (solved_leaf, solved_rows)


def solution(mesh):
    placed = (
        P(("row", "col"), None, None),
        P("col", None),
        P(("row", "col")),
        P(("row", "col"), None),
        P(("row", "col"), None, None),
        P(("row", "col"), None, None),
        P(("row", "col"), None, None),
        P(("row", "col"), None, None),
        P("row", "col"),
        P("row", "col"),
    )
    return jax.shard_map(
        shards,
        mesh=mesh,
        in_specs=placed,
        out_specs=(P(("row", "col"), None, None), P("row", None)),
        check_vma=False,
    )
```

profile of v0, /device:TPU:0, one launch (start us, length us, event | category | flops | bytes accessed | tf_op | source)
XLA Modules:
  0.0 286.2 jit_solution(5005880300283472320)
XLA Ops:
  7.2 0.0 copy-start
  7.2 0.0 all-reduce.2.cloned.1.call-start
  8.0 0.0 copy-start.1
  8.0 7.1 %fusion.9 = bf16[128,2048]{1,0:T(8,128)(2,1)S(1)} fusion(bf16[1,2048,2048]{2,1,0:T(8,128)(2,1)} %param.14, bf16[1,2048,128]{2,1,0:T(8,128)(2,1)} %param.10, pred[2048]{0:T(1024)(128)(4,1)S(1)} %iota_compare_fusion), kind=kOutput, calls=%fused_computation.9 | convolution fusion | flops 1074528256 | bytes 9439232 | tf_op jit(solution)/shard_map/lij,ljk->lik/dot_general | solution.py:30
  15.1 0.0 copy-start.5
  15.1 0.8 fusion.24
  16.0 0.1 copy.14
  16.1 0.1 reshape.122
  16.2 0.0 copy-start.2
  16.2 1.8 fusion.38
  18.0 2.4 reshape.123
  20.4 0.0 all-reduce.2.cloned.1.call-update
  20.5 149.3 %all-reduce.2.cloned.1.call-done = f32[2048,128]{1,0:T(8,128)} async-done(((f32[2048,128]{1,0:T(8,128)}), f32[2048,128]{1,0:T(8,128)}) %all-reduce.2.cloned.1.call-update) | async-done | bytes 1048592 | tf_op jit(solution)/shard_map/psum | solution.py:41
  169.7 1.1 convolution_bitcast_fusion.1
  170.8 25.9 %psum.22 = bf16[128,128]{0,1:T(8,128)(2,1)S(1)} all-reduce(f32[128,128]{0,1:T(8,128)S(1)} %convolution_bitcast_fusion.1), channel_id=1, replica_groups=mesh['row'=16,'col'=8] {'col'}, use_global_device_ids=true, to_apply=%region_1.2 | all-reduce | flops 16384 | bytes 98304 | tf_op jit(solution)/shard_map/psum | solution.py:45
  196.7 23.9 %all_gather.6 = bf16[2048,128]{0,1:T(8,128)(2,1)S(1)} all-gather(bf16[128,128]{0,1:T(8,128)(2,1)S(1)} %psum.22), channel_id=1, replica_groups=mesh['row'=16,'col'=8] {'row'}, dimensions={0}, use_global_device_ids=true | all-gather | bytes 557056 | tf_op jit(solution)/shard_map/all_gather | solution.py:46
  220.7 0.1 convolution_bitcast_fusion
  220.8 24.0 %psum.23 = bf16[128,128]{0,1:T(8,128)(2,1)S(1)} all-reduce(f32[128,128]{0,1:T(8,128)S(1)} %convolution_bitcast_fusion), channel_id=1, replica_groups=mesh['row'=16,'col'=8] {'col'}, use_global_device_ids=true, to_apply=%region_2.3 | all-reduce | flops 16384 | bytes 98304 | tf_op jit(solution)/shard_map/psum | solution.py:49
  244.8 23.2 %all_gather.7 = bf16[2048,128]{0,1:T(8,128)(2,1)S(1)} all-gather(bf16[128,128]{0,1:T(8,128)(2,1)S(1)} %psum.23), channel_id=1, replica_groups=mesh['row'=16,'col'=8] {'row'}, dimensions={0}, use_global_device_ids=true | all-gather | bytes 557056 | tf_op jit(solution)/shard_map/all_gather | solution.py:50
  268.0 0.7 copy.17
  268.7 1.0 copy.18
  269.7 1.6 gather_fusion
  271.3 7.0 %fusion.18 = bf16[1,2048,128]{1,2,0:T(8,128)(2,1)S(1)} fusion(bf16[1,2048,2048]{2,1,0:T(8,128)(2,1)} %param.15, bf16[512,128]{1,0:T(8,128)(2,1)S(1)} %bitcast.55, bf16[1,2048,512]{2,1,0:T(8,128)(2,1)S(1)} %copy-done, bf16[128,2048]{1,0:T(8,128)(2,1)S(1)} %fusion.9, pred[2048]{0:T(1024)(128)(4,1)S(1)} %iota_compare_fusion), kind=kOutput, calls=%fused_computation.12 | convolution fusion | flops 1343750144 | bytes 11667456 | tf_op jit(solution)/shard_map/lij,ljk->lik/dot_general | solution.py:57
  278.3 1.0 copy.16
  (11 shorter events, 0.0 us)
Async XLA Ops:
  7.2 264.2 %copy-start = (bf16[1,2048,512]{2,1,0:T(8,128)(2,1)S(1)}, bf16[1,2048,512]{2,1,0:T(8,128)(2,1)}, u32[]{:S(2)}) copy-start(bf16[1,2048,512]{2,1,0:T(8,128)(2,1)} %param.17) | copy-start | bytes 6291460
  7.2 162.5 %all-reduce.2.cloned.1.call-start = ((), (), s32[]{:S(2)}) async-start(), calls=%async_computation | async-start | bytes 2097152 | tf_op jit(solution)/shard_map/psum | solution.py:41
  8.0 7.1 %copy-start.1 = (bf16[1,512,2048]{2,1,0:T(8,128)(2,1)S(1)}, bf16[1,512,2048]{2,1,0:T(8,128)(2,1)}, u32[]{:S(2)}) copy-start(bf16[1,512,2048]{2,1,0:T(8,128)(2,1)} %param.16) | copy-start | bytes 6291460
  15.1 1.1 copy-start.5
  16.2 153.5 %copy-start.2 = (bf16[128,256]{1,0:T(8,128)(2,1)S(1)}, bf16[128,256]{1,0:T(8,128)(2,1)}, u32[]{:S(2)}) copy-start(bf16[128,256]{1,0:T(8,128)(2,1)} %param.18) | copy-start | bytes 196612
  16.2 153.5 %copy-start.3 = (bf16[256,128]{1,0:T(8,128)(2,1)S(1)}, bf16[256,128]{1,0:T(8,128)(2,1)}, u32[]{:S(2)}) copy-start(bf16[256,128]{1,0:T(8,128)(2,1)} %param.11) | copy-start | bytes 196612
  18.0 202.7 %copy-start.4 = (bf16[128,256]{1,0:T(8,128)(2,1)S(1)}, bf16[128,256]{1,0:T(8,128)(2,1)}, u32[]{:S(2)}) copy-start(bf16[128,256]{1,0:T(8,128)(2,1)} %param.19) | copy-start | bytes 196612
Sparse Core Ops, SparseCore 0:
  20.5 149.1 all-reduce.1
where the time goes:
time: 286 us
  waiting for transfers between devices  149 us (52%)
  blocking collectives  97 us (34%)
  matrix products  17.8 us (6%)
  between operations  15 us (5%)
  local copies, waits for them, and re-layouts  7.01 us (2%)
    psum x1, waiting for transfers between devices, shards(): coupled_sum = lax.psum(partial_sum, ('row', 'col'))  149 us
    psum x1, blocking collectives, shards(): forward_rows = lax.psum(forward_terms, 'col').astype(jnp.bfloat16)  25.9 us
    psum x1, blocking collectives, shards(): solved_rows = lax.psum(solved_terms, 'col').astype(jnp.bfloat16)  24 us
    all_gather x1, blocking collectives, shards(): sep_forward = lax.all_gather(forward_rows, 'row', axis=0, tiled=True)  23.9 us
    all_gather x1, blocking collectives, shards(): solved_sep = lax.all_gather(solved_rows, 'row', axis=0, tiled=True)  23.2 us
    dot_general x1, matrix products, shards(): jnp.einsum('lij,ljk->lik', linv_leaf, masked, preferred_element_type=jnp....  7.05 us
    dot_general x1, matrix products, shards(): jnp.einsum('lij,ljk->lik', uinv_leaf, residue, preferred_element_type=jnp...  6.96 us
  transfers between devices with their start and end apart: 1, of which 1 were waited for; matrix products, arithmetic and copies ran while one was open for 0% of the time, Pallas kernels for 0%

commit v1 on v0

v1 whole, which is shorter than its diff:
```python
import jax
import jax.numpy as jnp
from jax import lax
from jax.experimental import pallas as pl
from jax.experimental.pallas import tpu as pltpu
from jax.sharding import PartitionSpec as P

MESH = pl.DeviceIdType.MESH
W = 2048
NR = 128
BLK = 128
KB = 4
TB = 256
NT = W // TB
BF = jnp.bfloat16
F32 = jnp.float32
CLASSES = ((96, 64, "xyz"), (0, 48, "yzx"), (48, 48, "zxy"))
SLOT = 160


def dot(a, b):
    return jnp.dot(a, b, preferred_element_type=F32)


def kernel(
    sizes, offs, rhs_h, rsep_h, linv_h, uinv_h, loff_h, uoff_h, lsep_h, usep_h,
    out_h, osep_h,
    linv, uinv, loff, rhs, mix, gmat, fsol, upd, slots, rsep,
    half, recv_half, pieces, rs_in, xs, pf_send, pf_recv, fwd_sep, ps, pr, coupled, obuf, osep,
    s_rhs, s_linv, s_loff, s_uinv, s_uoff, s_own, s_diag, s_rsep, s_out, s_osep,
    ph_send, ph_recv, dg_send, dg_recv, core_send, core_recv, rs_send, rs_recv, ag_send, ag_recv,
    sem_a, sem_b,
):
    row, col = lax.axis_index("row"), lax.axis_index("col")
    z, y = row // 4, row % 4
    x, k = col // 2, col % 2
    other = 1 - k
    chip = z * 16 + y * 4 + x
    size = sizes[0]
    partner = (row, x * 2 + other)

    def line(dim, step):
        if dim == "z":
            return (((z + step) % 4) * 4 + y, col)
        if dim == "y":
            return (z * 4 + (y + step) % 4, col)
        return (row, ((x + step) % 4) * 2 + k)

    def wait_bytes(ref, sem):
        pltpu.make_async_copy(ref, ref, sem).wait()

    def keep(start, rows, cols):
        return lax.broadcasted_iota(jnp.int32, (rows, cols), 0) + start < size

    barrier = pltpu.get_barrier_semaphore()
    pl.semaphore_signal(barrier, inc=1, device_id=partner, device_id_type=MESH)
    for dim in "xyz":
        for step in (1, 2, 3):
            pl.semaphore_signal(barrier, inc=1, device_id=line(dim, step), device_id_type=MESH)

    def rows_of(i):
        return pl.ds(TB * i, TB)

    pltpu.make_async_copy(rhs_h.at[0], rhs, s_rhs).start()
    own = slots.at[z, y, x, pl.ds(0, BLK)]

    def load_front(i):
        pltpu.make_async_copy(
            linv_h.at[0, rows_of(i), pl.ds(0, TB * (i + 1))],
            linv.at[rows_of(i), pl.ds(0, TB * (i + 1))], s_linv.at[i]).start()
        pltpu.make_async_copy(
            loff_h.at[0, :, rows_of(i)], loff.at[:, rows_of(i)], s_loff.at[i]).start()

    load_front(7)

    @pl.when(x <= z)
    def _():
        pltpu.make_async_copy(lsep_h, own, s_own).start()

    @pl.when(x > z)
    def _():
        pltpu.make_async_copy(usep_h, own, s_own).start()

    @pl.when(x == z)
    def _():
        for j in range(4):
            pltpu.make_async_copy(
                usep_h.at[pl.ds(32 * j, 32)], slots.at[z, y, j, pl.ds(BLK, 32)], s_diag).start()

    for i in range(6, -1, -1):
        load_front(i)
    pltpu.make_async_copy(rsep_h, rsep, s_rsep).start()

    wait_bytes(rhs, s_rhs)
    for i in range(NT):
        part = rhs[rows_of(i), :].astype(F32)
        rhs[rows_of(i), :] = jnp.where(keep(TB * i, TB, NR), part, 0.0).astype(BF)

    total = [None]

    def front(i):
        span = pl.ds(0, TB * (i + 1))
        wait_bytes(linv.at[rows_of(i), span], s_linv.at[i])
        part = dot(linv[rows_of(i), span], rhs[span, :])
        part = jnp.where(keep(TB * i, TB, NR), part, 0.0).astype(BF)
        mix[rows_of(i), pl.ds(KB * BLK, NR)] = part
        wait_bytes(loff.at[:, rows_of(i)], s_loff.at[i])
        term = dot(loff[:, rows_of(i)], part)
        total[0] = term if total[0] is None else total[0] + term

    def region(ph, order, first, rows):
        have = order[:ph]
        return slots.at[
            slice(None) if "z" in have else z,
            slice(None) if "y" in have else y,
            slice(None) if "x" in have else x,
            pl.ds(first, rows)]

    def three(ph, first, rows):
        if ph == 0:
            return slots.at[0, 0, pl.ds(0, 3), pl.ds(first, rows)]
        if ph == 1:
            return slots.at[0, pl.ds(0, 3), :, pl.ds(first, rows)]
        return slots.at[pl.ds(0, 3), :, :, pl.ds(first, rows)]

    def span_of(ph, cl):
        first, rows, order = CLASSES[cl]
        if ph == 0 and cl == 0:
            rows = BLK - first
        return first, rows, order

    def phase_start(ph):
        for cl in range(3):
            first, rows, order = span_of(ph, cl)
            ref = region(ph, order, first, rows)
            for step in (2, 1, 3):
                pltpu.make_async_remote_copy(
                    src_ref=ref, dst_ref=ref, send_sem=ph_send.at[ph, cl], recv_sem=ph_recv.at[ph, cl],
                    device_id=line(order[ph], step), device_id_type=MESH).start()
        if ph == 0:
            @pl.when(x == z)
            def _():
                ref = slots.at[z, y, :, pl.ds(BLK, 32)]
                for step in (2, 1, 3):
                    pltpu.make_async_remote_copy(
                        src_ref=ref, dst_ref=ref, send_sem=dg_send, recv_sem=dg_recv,
                        device_id=line("x", step), device_id_type=MESH).start()

    def phase_wait(ph):
        for cl in range(3):
            first, rows, _ = span_of(ph, cl)
            wait_bytes(three(ph, first, rows), ph_recv.at[ph, cl])
        if ph == 0:
            @pl.when(x != z)
            def _():
                wait_bytes(slots.at[0, 0, :, pl.ds(BLK, 32)], dg_recv)

    def phase_drain(ph):
        for cl in range(3):
            first, rows, _ = span_of(ph, cl)
            wait_bytes(three(ph, first, rows), ph_send.at[ph, cl])
        if ph == 0:
            @pl.when(x == z)
            def _():
                wait_bytes(slots.at[0, pl.ds(0, 3), :, pl.ds(BLK, 32)], dg_send)

    front(7)
    wait_bytes(own, s_own)

    @pl.when(x == z)
    def _():
        wait_bytes(slots.at[0, 0, :, pl.ds(BLK, 32)], s_diag)

    pl.semaphore_wait(barrier, 10)
    for step in (1, 2, 3):
        pl.semaphore_signal(sem_a, inc=1, device_id=line("x", step), device_id_type=MESH)
    phase_start(0)
    for i in (6, 5, 4):
        front(i)
    pltpu.make_async_copy(
        uoff_h.at[0], mix.at[:, pl.ds(0, KB * BLK)], s_uoff).start()
    for i in range(NT):
        span = pl.ds(TB * i, W - TB * i)
        pltpu.make_async_copy(
            uinv_h.at[0, rows_of(i), span], uinv.at[rows_of(i), span], s_uinv.at[i]).start()
    pl.semaphore_wait(sem_a, 3)
    for step in (1, 2, 3):
        pl.semaphore_signal(sem_b, inc=1, device_id=line("y", step), device_id_type=MESH)
    for i in (3, 2, 1, 0):
        front(i)

    for j in range(KB):
        upd[j] = total[0][BLK * j:BLK * (j + 1), :].reshape(8, 16, NR).astype(BF)
    upd[KB] = jnp.zeros((8, 16, NR), BF)
    named = [offs[0, j] for j in range(KB)]

    def block(s):
        at = jnp.int32(KB)
        for j in range(KB):
            at = jnp.where(named[j] == s, j, at)
        return upd[at]

    for c4 in range(4):
        for b in range(2):
            half[c4, pl.ds(8 * b, 8)] = block(4 * c4 + 2 * other + b)
    swap = pltpu.make_async_remote_copy(
        src_ref=half, dst_ref=recv_half, send_sem=core_send.at[0], recv_sem=core_recv.at[0],
        device_id=partner, device_id_type=MESH)
    swap.start()
    phase_wait(0)
    phase_start(1)
    pl.semaphore_wait(sem_b, 3)
    swap.wait_recv()
    for c4 in range(4):
        for b in range(2):
            mine = block(4 * c4 + 2 * k + b).astype(F32)
            got = recv_half[c4, pl.ds(8 * b, 8)].astype(F32)
            pieces[pl.ds(16 * c4 + 8 * b, 8)] = (mine + got).astype(BF)

    def peer(i):
        dz, dy, dx = (i // 16 + 2) % 4, (i // 4 + 2) % 4, (i + 2) % 4
        pz, py, px = (z + dz) % 4, (y + dy) % 4, (x + dx) % 4
        return pz * 4 + py, px

    def rs_body(i, carry):
        @pl.when(i != 42)
        def _():
            prow, px = peer(i)
            pltpu.make_async_remote_copy(
                src_ref=pieces.at[px * 16 + prow], dst_ref=rs_in.at[chip], send_sem=rs_send, recv_sem=rs_recv,
                device_id=(prow, px * 2 + k), device_id_type=MESH).start()
        return carry

    lax.fori_loop(0, 64, rs_body, 0)
    rs_in[chip] = pieces[x * 16 + row]

    wait_bytes(mix.at[:, pl.ds(0, KB * BLK)], s_uoff)
    for i in range(NT):
        part = mix[rows_of(i), pl.ds(0, KB * BLK)].astype(F32)
        mix[rows_of(i), pl.ds(0, KB * BLK)] = jnp.where(keep(TB * i, TB, KB * BLK), part, 0.0).astype(BF)

    def back(i):
        span = pl.ds(TB * i, W - TB * i)
        wait_bytes(uinv.at[rows_of(i), span], s_uinv.at[i])
        gmat[rows_of(i), :] = dot(uinv[rows_of(i), span], mix[span, pl.ds(0, KB * BLK)]).astype(BF)
        fsol[rows_of(i), :] = dot(uinv[rows_of(i), span], mix[span, pl.ds(KB * BLK, NR)])

    back(0)
    back(1)
    phase_wait(1)
    phase_start(2)
    wait_bytes(rsep, s_rsep)
    wait_bytes(rs_in.at[pl.ds(0, 63)], rs_recv)
    gathered = jnp.sum(rs_in[...].astype(F32), axis=0)
    xs[x * 16 + row] = (rsep[pl.ds(pl.multiple_of(row * 16, 16), 16), :].astype(F32) - gathered).astype(BF)

    def ag_body(i, carry):
        @pl.when(i != 42)
        def _():
            prow, px = peer(i)
            pltpu.make_async_remote_copy(
                src_ref=xs.at[x * 16 + row], dst_ref=xs.at[x * 16 + row], send_sem=ag_send, recv_sem=ag_recv,
                device_id=(prow, px * 2 + k), device_id_type=MESH).start()
        return carry

    lax.fori_loop(0, 64, ag_body, 0)
    for i in range(2, NT):
        back(i)
    wait_bytes(rs_in.at[pl.ds(0, 63)], ag_recv)
    phase_wait(2)

    def part_forward(z4, y4):
        acc = None
        for j in range(z4 + 1):
            term = dot(slots[z4, y4, j, pl.ds(0, BLK), :], xs[pl.ds(16 * j, 16)].reshape(TB, NR))
            acc = term if acc is None else acc + term
        return acc

    for z4 in range(4):
        for b in range(2):
            pf_send[z4, pl.ds(BLK * b, BLK)] = part_forward(z4, 2 * other + b).astype(BF)
    swap_f = pltpu.make_async_remote_copy(
        src_ref=pf_send, dst_ref=pf_recv, send_sem=core_send.at[1], recv_sem=core_recv.at[1],
        device_id=partner, device_id_type=MESH)
    swap_f.start()
    held = [[part_forward(z4, 2 * k + b) for b in range(2)] for z4 in range(4)]
    swap_f.wait_recv()
    for z4 in range(4):
        for b in range(2):
            fwd_sep[z4, pl.ds(BLK * b, BLK)] = (
                held[z4][b] + pf_recv[z4, pl.ds(BLK * b, BLK)].astype(F32)).astype(BF)

    swaps = []
    for z4 in (3, 2, 1, 0):
        for y4 in range(4):
            acc = dot(slots[z4, y4, :, pl.ds(BLK, 32), :].reshape(BLK, TB), fwd_sep[z4])
            for j in range(z4 + 1, 4):
                acc = acc + dot(slots[z4, y4, j, pl.ds(0, BLK), :], fwd_sep[j])
            ps[4 * z4 + y4] = acc.astype(BF)
        swaps.append(pltpu.make_async_remote_copy(
            src_ref=ps.at[pl.ds(4 * z4, 4)], dst_ref=pr.at[pl.ds(4 * z4, 4)],
            send_sem=core_send.at[2 + z4], recv_sem=core_recv.at[2 + z4],
            device_id=partner, device_id_type=MESH))
        swaps[-1].start()
    for s in swaps:
        s.wait_recv()

    def solved(s):
        return (ps[s].astype(F32) + pr[s].astype(F32)).astype(BF)

    osep[...] = solved(row)
    out_sep = pltpu.make_async_copy(osep, osep_h, s_osep)
    out_sep.start()
    for j in range(KB):
        coupled[pl.ds(BLK * j, BLK), :] = solved(named[j])
    outs = []
    for i in range(NT):
        part = fsol[rows_of(i), :] - dot(gmat[rows_of(i), :], coupled[...])
        obuf[rows_of(i), :] = jnp.where(keep(TB * i, TB, NR), part, 0.0).astype(BF)
        outs.append(pltpu.make_async_copy(obuf.at[rows_of(i)], out_h.at[0, rows_of(i)], s_out.at[i]))
        outs[-1].start()

    swap.wait_send()
    swap_f.wait_send()
    for s in swaps:
        s.wait_send()
    wait_bytes(rs_in.at[pl.ds(0, 63)], rs_send)
    wait_bytes(rs_in.at[pl.ds(0, 63)], ag_send)
    for ph in range(3):
        phase_drain(ph)
    out_sep.wait()
    for o in outs:
        o.wait()


def shards(
    rhs_leaf, rhs_sep, leaf_sizes, off_blocks, linv_leaf, uinv_leaf, l_off, u_off, linv_sep, uinv_sep,
):
    any_spec = pl.BlockSpec(memory_space=pl.ANY)
    smem = pl.BlockSpec(memory_space=pltpu.SMEM)
    dma = pltpu.SemaphoreType.DMA
    vm = pltpu.VMEM
    return pl.pallas_call(
        kernel,
        out_shape=(
            jax.ShapeDtypeStruct((1, W, NR), BF),
            jax.ShapeDtypeStruct((BLK, NR), BF),
        ),
        in_specs=[smem, smem] + [any_spec] * 8,
        out_specs=(any_spec, any_spec),
        scratch_shapes=[
            vm((W, W), BF), vm((W, W), BF), vm((KB * BLK, W), BF), vm((W, NR), BF),
            vm((W, KB * BLK + NR), BF), vm((W, KB * BLK), BF), vm((W, NR), F32),
            vm((KB + 1, 8, 16, NR), BF), vm((4, 4, 4, SLOT, TB), BF), vm((TB, NR), BF),
            vm((4, 16, 16, NR), BF), vm((4, 16, 16, NR), BF), vm((64, 16, NR), BF),
            vm((64, 16, NR), BF), vm((64, 16, NR), BF),
            vm((4, TB, NR), BF), vm((4, TB, NR), BF), vm((4, TB, NR), BF),
            vm((16, BLK, NR), BF), vm((16, BLK, NR), BF), vm((KB * BLK, NR), BF),
            vm((W, NR), BF), vm((BLK, NR), BF),
            dma, dma((NT,)), dma((NT,)), dma((NT,)), dma, dma, dma, dma, dma((NT,)), dma,
            dma((3, 3)), dma((3, 3)), dma, dma, dma((6,)), dma((6,)), dma, dma, dma, dma,
            pltpu.SemaphoreType.REGULAR, pltpu.SemaphoreType.REGULAR,
        ],
        compiler_params=pltpu.CompilerParams(
            collective_id=0, has_side_effects=True, vmem_limit_bytes=56 * 1024 * 1024),
        name="supernodal_solve",
    )(leaf_sizes, off_blocks, rhs_leaf, rhs_sep, linv_leaf, uinv_leaf, l_off, u_off, linv_sep, uinv_sep)


def solution(mesh):
    placed = (
        P(("row", "col"), None, None),
        P("col", None),
        P(("row", "col")),
        P(("row", "col"), None),
        P(("row", "col"), None, None),
        P(("row", "col"), None, None),
        P(("row", "col"), None, None),
        P(("row", "col"), None, None),
        P("row", "col"),
        P("row", "col"),
    )
    return jax.shard_map(
        shards,
        mesh=mesh,
        in_specs=placed,
        out_specs=(P(("row", "col"), None, None), P("row", None)),
        check_vma=False,
    )
```

time: 286 us -> 61.6 us (0.22)
  the two profiles are of different devices: /device:TPU:0 before, /device:TPU:1 now
where the time goes in v1:
time: 61.6 us; the launch traced here: 61.4 us
  Pallas kernels  56.9 us (92%)
  local copies, waits for them, and re-layouts  3.24 us (5%)
  between operations  1.29 us (2%)
    pallas_call x1, Pallas kernels, shards(): pl.pallas_call(kernel, out_shape=(jax.ShapeDtypeStruct((1, W, NR), BF), j...  56.9 us
    unnamed x2, local copies, waits for them, and re-layouts  3.24 us

profile of v1, /device:TPU:1, one launch (start us, length us, event | category | flops | bytes accessed | tf_op | source)
XLA Modules:
  0.0 61.4 jit_solution(9633363562474449351)
XLA Ops:
  1.3 56.9 %supernodal_solve.1 = (bf16[1,2048,128]{2,1,0:T(8,128)(2,1)}, bf16[128,128]{1,0:T(8,128)(2,1)}) custom-call(s32[1]{0:T(128)S(6)} %copy.14.sizes, s32[1,4]{1,0:T(1,128)} %offs.1, bf16[1,2048,128]{2,1,0:T(8,128)(2,1)} %rhs_h.1, bf16[256,128]{1,0:T(8,128)(2,1)} %rsep_h.1, bf16[1,2048,2048]{2,1,0:T(8,128)(2,1)} %linv_h.1, bf16[1,2048,2048]{2,1,0:T(8,128)(2,1)} %uinv_h.1, ...), custom_call_target="tpu_custom_call" | custom-call | tf_op jit(solution)/shard_map/supernodal_solve/pallas_call | solution.py:343
  58.2 1.9 %copy.15 = bf16[1,2048,128]{2,1,0:T(8,128)(2,1)} copy(bf16[1,2048,128]{2,1,0:T(8,128)(2,1)} %get-tuple-element.4) | data formatting | bytes 1048576
  60.0 1.4 %copy.16 = bf16[128,128]{1,0:T(8,128)(2,1)} copy(bf16[128,128]{1,0:T(8,128)(2,1)} %get-tuple-element.5) | data formatting | bytes 65536

commit v2 on v0

v2 whole, which is shorter than its diff:
```python
import jax
import jax.numpy as jnp
from jax import lax
from jax.experimental import pallas as pl
from jax.experimental.pallas import tpu as pltpu
from jax.sharding import PartitionSpec as P

MESH = pl.DeviceIdType.MESH
W = 2048
NR = 128
BLK = 128
KB = 4
TB = 256
NT = W // TB
WINDOW = 3
BF = jnp.bfloat16
F32 = jnp.float32


def dot(a, b):
    return jnp.dot(a, b, preferred_element_type=F32)


def kernel(
    sizes, offs, rhs_h, rsep_h, linv_h, uinv_h, loff_h, uoff_h, lsep_h, usep_h,
    out_h, osep_h,
    linv, uinv, loff, rhs, mix, gmat, fsol, upd, rsep,
    lcol, urow, macc, mout, mrow,
    half, recv_half, pieces, rs_in, xs, part, part_in, sol, coupled, obuf, osep,
    s_rhs, s_linv, s_loff, s_uinv, s_uoff, s_own, s_rsep, s_out, s_osep,
    l_send, l_recv, u_send, u_recv, uc_sem, m_send, m_recv,
    core_send, core_recv, rs_send, rs_recv, ag_send, ag_recv,
    sem_a,
):
    row, col = lax.axis_index("row"), lax.axis_index("col")
    z, y = row // 4, row % 4
    x, k = col // 2, col % 2
    other = 1 - k
    chip = z * 16 + y * 4 + x
    size = sizes[0]
    partner = (row, x * 2 + other)

    def along_x(step):
        return (row, ((x + step) % 4) * 2 + k)

    def wait_bytes(ref, sem):
        pltpu.make_async_copy(ref, ref, sem).wait()

    def remote(src, dst, send, recv, device):
        return pltpu.make_async_remote_copy(
            src_ref=src, dst_ref=dst, send_sem=send, recv_sem=recv,
            device_id=device, device_id_type=MESH)

    def keep(start, rows, cols):
        return lax.broadcasted_iota(jnp.int32, (rows, cols), 0) + start < size

    def rows_of(i):
        return pl.ds(TB * i, TB)

    def load_front(i):
        pltpu.make_async_copy(rhs_h.at[0, rows_of(i)], rhs.at[rows_of(i)], s_rhs.at[i]).start()
        span = pl.ds(0, TB * (i + 1))
        pltpu.make_async_copy(
            linv_h.at[0, rows_of(i), span], linv.at[rows_of(i), span], s_linv.at[i]).start()
        pltpu.make_async_copy(
            loff_h.at[0, :, rows_of(i)], loff.at[:, rows_of(i)], s_loff.at[i]).start()

    for i in range(WINDOW):
        load_front(i)

    barrier = pltpu.get_barrier_semaphore()

    def greet(i, carry):
        pl.semaphore_signal(barrier, inc=1, device_id=((row + i) % 16, col), device_id_type=MESH)
        return carry

    for step in (1, 2, 3):
        pl.semaphore_signal(barrier, inc=1, device_id=along_x(step), device_id_type=MESH)
    pl.semaphore_signal(barrier, inc=1, device_id=partner, device_id_type=MESH)
    lax.fori_loop(1, 16, greet, 0)

    pltpu.make_async_copy(lsep_h, lcol.at[row], s_own.at[0]).start()
    pltpu.make_async_copy(usep_h, urow.at[k, x], s_own.at[1]).start()
    pltpu.make_async_copy(rsep_h, rsep, s_rsep).start()

    total = [None]

    def front(i):
        span = pl.ds(0, TB * (i + 1))
        wait_bytes(rhs.at[rows_of(i)], s_rhs.at[i])
        wait_bytes(linv.at[rows_of(i), span], s_linv.at[i])
        if i + WINDOW < NT:
            load_front(i + WINDOW)
        mask = keep(TB * i, TB, NR)
        rhs[rows_of(i), :] = jnp.where(mask, rhs[rows_of(i), :].astype(F32), 0.0).astype(BF)
        val = dot(linv[rows_of(i), span], rhs[span, :])
        val = jnp.where(mask, val, 0.0).astype(BF)
        mix[rows_of(i), pl.ds(KB * BLK, NR)] = val
        wait_bytes(loff.at[:, rows_of(i)], s_loff.at[i])
        term = dot(loff[:, rows_of(i)], val)
        total[0] = term if total[0] is None else total[0] + term

    for i in range(NT - 2):
        front(i)

    pl.semaphore_wait(barrier, 19)
    for step in (1, 2, 3):
        pl.semaphore_signal(sem_a, inc=1, device_id=along_x(step), device_id_type=MESH)
    wait_bytes(lcol.at[row], s_own.at[0])
    wait_bytes(urow.at[k, x], s_own.at[1])
    for step in (2, 1, 3):
        remote(urow.at[k, x], urow.at[k, x], u_send, u_recv, along_x(step)).start()
    filled = row >= 2 * col

    @pl.when(filled)
    def _():
        def body(i, carry):
            remote(lcol.at[row], lcol.at[row], l_send, l_recv.at[row], ((row + i) % 16, col)).start()
            return carry

        lax.fori_loop(1, 16, body, 0)

    for i in range(NT - 2, NT):
        front(i)
    pltpu.make_async_copy(
        uoff_h.at[0], mix.at[:, pl.ds(0, KB * BLK)], s_uoff).start()
    for i in range(NT):
        span = pl.ds(TB * i, W - TB * i)
        pltpu.make_async_copy(
            uinv_h.at[0, rows_of(i), span], uinv.at[rows_of(i), span], s_uinv.at[i]).start()

    for j in range(KB):
        upd[j] = total[0][BLK * j:BLK * (j + 1), :].reshape(8, 16, NR).astype(BF)
    upd[KB] = jnp.zeros((8, 16, NR), BF)
    named = [offs[0, j] for j in range(KB)]

    def block(s):
        at = jnp.int32(KB)
        for j in range(KB):
            at = jnp.where(named[j] == s, j, at)
        return upd[at]

    swaps = []
    for j in range(4):
        c4 = (x + 2 + j) % 4
        for b in range(2):
            half[j, pl.ds(8 * b, 8)] = block(4 * c4 + 2 * other + b)
        swaps.append(remote(half.at[j], recv_half.at[j], core_send.at[j], core_recv.at[j], partner))
        swaps[-1].start()
    pl.semaphore_wait(sem_a, 3)
    for j in range(4):
        c4 = (x + 2 + j) % 4
        swaps[j].wait_recv()
        for b in range(2):
            mine = block(4 * c4 + 2 * k + b).astype(F32)
            got = recv_half[j, pl.ds(8 * b, 8)].astype(F32)
            pieces[c4, pl.ds(8 * b, 8)] = (mine + got).astype(BF)

        def rs_body(i, carry, c4=c4):
            prow = ((z + i // 4 + 2) % 4) * 4 + (y + i + 2) % 4
            remote(pieces.at[c4, prow], rs_in.at[chip], rs_send, rs_recv, (prow, c4 * 2 + k)).start()
            return carry

        if j == 2:
            lax.fori_loop(0, 10, rs_body, 0)
            lax.fori_loop(11, 16, rs_body, 0)
            rs_in[chip] = pieces[c4, row]
        else:
            lax.fori_loop(0, 16, rs_body, 0)

    wait_bytes(urow.at[0, pl.ds(0, 3)], u_recv)
    give_u = remote(urow.at[k], urow.at[k], uc_sem.at[0], uc_sem.at[1], partner)
    give_u.start()

    wait_bytes(mix.at[:, pl.ds(0, KB * BLK)], s_uoff)
    for i in range(NT):
        val = mix[rows_of(i), pl.ds(0, KB * BLK)].astype(F32)
        mix[rows_of(i), pl.ds(0, KB * BLK)] = jnp.where(keep(TB * i, TB, KB * BLK), val, 0.0).astype(BF)

    def back(i):
        span = pl.ds(TB * i, W - TB * i)
        wait_bytes(uinv.at[rows_of(i), span], s_uinv.at[i])
        gmat[rows_of(i), :] = dot(uinv[rows_of(i), span], mix[span, pl.ds(0, KB * BLK)]).astype(BF)
        fsol[rows_of(i), :] = dot(uinv[rows_of(i), span], mix[span, pl.ds(KB * BLK, NR)])

    back(0)
    give_u.wait_recv()

    def l_wait(i, carry):
        @pl.when(i != row)
        def _():
            wait_bytes(lcol.at[i], l_recv.at[i])
        return carry

    lax.fori_loop(2 * col, 16, l_wait, 0)
    macc[...] = jnp.zeros_like(macc)

    def m_body(c, carry):
        macc[...] += dot(urow[c % 2, c // 2], lcol[pl.ds(2 * c, 2)].reshape(TB, TB))
        return carry

    lax.fori_loop(jnp.maximum(col, row // 2), 8, m_body, 0)
    mout[...] = macc[...].reshape(4, 32, TB).astype(BF)
    for step in (2, 1, 3):
        px = (x + step) % 4
        remote(mout.at[px], mrow.at[x], m_send, m_recv, along_x(step)).start()
    mrow[x] = mout[x]
    back(1)

    wait_bytes(rsep, s_rsep)
    wait_bytes(rs_in.at[pl.ds(0, 63)], rs_recv)
    gathered = jnp.sum(rs_in[...].astype(F32), axis=0)
    xs[x * 16 + row] = (rsep[pl.ds(pl.multiple_of(row * 16, 16), 16), :].astype(F32) - gathered).astype(BF)

    def spread(ref, sem):
        def body(i, carry):
            pz, py, px = (z + i // 16 + 2) % 4, (y + i // 4 + 2) % 4, (x + i + 2) % 4
            remote(ref, ref, ag_send.at[sem], ag_recv.at[sem], (pz * 4 + py, px * 2 + k)).start()
            return carry

        lax.fori_loop(0, 42, body, 0)
        lax.fori_loop(43, 64, body, 0)

    spread(xs.at[x * 16 + row], 0)
    for i in range(2, 5):
        back(i)
    wait_bytes(mrow.at[pl.ds(0, 3)], m_recv)
    wait_bytes(rs_in.at[pl.ds(0, 63)], ag_recv.at[0])

    val = None
    for j in range(4):
        term = dot(mrow[j], xs[pl.ds(16 * j, 16)].reshape(TB, NR))
        val = term if val is None else val + term
    part[...] = val.reshape(2, 16, NR)
    swap_m = remote(part.at[other], part_in, core_send.at[4], core_recv.at[4], partner)
    swap_m.start()
    swap_m.wait_recv()
    sol[k, row, x] = (part[k] + part_in[...]).astype(BF)
    spread(sol.at[k, row, x], 1)
    for i in range(5, NT):
        back(i)
    wait_bytes(rs_in.at[pl.ds(0, 63)], ag_recv.at[1])
    swap_s = remote(sol.at[k], sol.at[k], core_send.at[5], core_recv.at[5], partner)
    swap_s.start()
    swap_s.wait_recv()

    for j in range(KB):
        for h in range(2):
            got = sol[h, named[j]]
            for q in range(4):
                coupled[pl.ds(BLK * j + 32 * q + 16 * h, 16), :] = got[q]
    outs = []
    for i in range(NT):
        val = fsol[rows_of(i), :] - dot(gmat[rows_of(i), :], coupled[...])
        obuf[rows_of(i), :] = jnp.where(keep(TB * i, TB, NR), val, 0.0).astype(BF)
        outs.append(pltpu.make_async_copy(obuf.at[rows_of(i)], out_h.at[0, rows_of(i)], s_out.at[i]))
        outs[-1].start()
    for h in range(2):
        got = sol[h, row]
        for q in range(4):
            osep[pl.ds(32 * q + 16 * h, 16), :] = got[q]
    outs.append(pltpu.make_async_copy(osep, osep_h, s_osep))
    outs[-1].start()

    for s in swaps + [swap_m, swap_s, give_u]:
        s.wait_send()
    wait_bytes(urow.at[0, pl.ds(0, 3)], u_send)
    wait_bytes(mrow.at[pl.ds(0, 3)], m_send)

    @pl.when(filled)
    def _():
        wait_bytes(lcol.at[pl.ds(0, 15)], l_send)

    for sem in (rs_send, ag_send.at[0], ag_send.at[1]):
        wait_bytes(rs_in.at[pl.ds(0, 63)], sem)
    for o in outs:
        o.wait()


def hand_over(leaf, sep, leaf_out, sep_out, sems):
    one = pltpu.make_async_copy(leaf, leaf_out, sems.at[0])
    two = pltpu.make_async_copy(sep, sep_out, sems.at[1])
    one.start()
    two.start()
    one.wait()
    two.wait()


def shards(
    rhs_leaf, rhs_sep, leaf_sizes, off_blocks, linv_leaf, uinv_leaf, l_off, u_off, linv_sep, uinv_sep,
):
    any_spec = pl.BlockSpec(memory_space=pl.ANY)
    smem = pl.BlockSpec(memory_space=pltpu.SMEM)
    dma = pltpu.SemaphoreType.DMA
    vm = pltpu.VMEM
    out_shape = (
        jax.ShapeDtypeStruct((1, W, NR), BF),
        jax.ShapeDtypeStruct((BLK, NR), BF),
    )
    solved = pl.pallas_call(
        kernel,
        out_shape=out_shape,
        in_specs=[smem, smem] + [any_spec] * 8,
        out_specs=(any_spec, any_spec),
        scratch_shapes=[
            vm((W, W), BF), vm((W, W), BF), vm((KB * BLK, W), BF), vm((W, NR), BF),
            vm((W, KB * BLK + NR), BF), vm((W, KB * BLK), BF), vm((W, NR), F32),
            vm((KB + 1, 8, 16, NR), BF), vm((TB, NR), BF),
            vm((16, BLK, TB), BF), vm((2, 4, BLK, TB), BF), vm((BLK, TB), F32),
            vm((4, 32, TB), BF), vm((4, 32, TB), BF),
            vm((4, 16, 16, NR), BF), vm((4, 16, 16, NR), BF), vm((4, 16, 16, NR), BF),
            vm((64, 16, NR), BF), vm((64, 16, NR), BF),
            vm((2, 16, NR), F32), vm((16, NR), F32), vm((2, 16, 4, 16, NR), BF),
            vm((KB * BLK, NR), BF), vm((W, NR), BF), vm((BLK, NR), BF),
            dma((NT,)), dma((NT,)), dma((NT,)), dma((NT,)), dma, dma((2,)), dma, dma((NT,)), dma,
            dma, dma((16,)), dma, dma, dma((2,)), dma, dma,
            dma((6,)), dma((6,)), dma, dma, dma((2,)), dma((2,)),
            pltpu.SemaphoreType.REGULAR,
        ],
        compiler_params=pltpu.CompilerParams(
            collective_id=0, has_side_effects=True, vmem_limit_bytes=56 * 1024 * 1024),
        name="supernodal_solve",
    )(leaf_sizes, off_blocks, rhs_leaf, rhs_sep, linv_leaf, uinv_leaf, l_off, u_off, linv_sep, uinv_sep)
    return pl.pallas_call(
        hand_over,
        out_shape=out_shape,
        in_specs=[any_spec, any_spec],
        out_specs=(any_spec, any_spec),
        scratch_shapes=[dma((2,))],
        compiler_params=pltpu.CompilerParams(vmem_limit_bytes=56 * 1024 * 1024),
        name="hand_over",
    )(*solved)


def solution(mesh):
    placed = (
        P(("row", "col"), None, None),
        P("col", None),
        P(("row", "col")),
        P(("row", "col"), None),
        P(("row", "col"), None, None),
        P(("row", "col"), None, None),
        P(("row", "col"), None, None),
        P(("row", "col"), None, None),
        P("row", "col"),
        P("row", "col"),
    )
    return jax.shard_map(
        shards,
        mesh=mesh,
        in_specs=placed,
        out_specs=(P(("row", "col"), None, None), P("row", None)),
        check_vma=False,
    )
```

time: 286 us -> 66.2 us (0.23)
  the two profiles are of different devices: /device:TPU:0 before, /device:TPU:1 now
where the time goes in v2:
time: 66.2 us; the launch traced here: 66 us
  Pallas kernels  64.8 us (98%)
  between operations  1.29 us (2%)
    pallas_call x1, Pallas kernels, shards(): pl.pallas_call(kernel, out_shape=out_shape, in_specs=[smem, smem] + [any_...  46.8 us
    pallas_call x1, Pallas kernels, shards(): pl.pallas_call(hand_over, out_shape=out_shape, in_specs=[any_spec, any_sp...  18 us

profile of v2, /device:TPU:1, one launch (start us, length us, event | category | flops | bytes accessed | tf_op | source)
XLA Modules:
  0.0 66.0 jit_solution(233691700159814177)
XLA Ops:
  1.3 46.8 %supernodal_solve.1 = (bf16[1,2048,128]{2,1,0:T(8,128)(2,1)}, bf16[128,128]{1,0:T(8,128)(2,1)}) custom-call(s32[1]{0:T(128)S(6)} %copy.12.sizes, s32[1,4]{1,0:T(1,128)} %offs.1, bf16[1,2048,128]{2,1,0:T(8,128)(2,1)} %rhs_h.1, bf16[256,128]{1,0:T(8,128)(2,1)} %rsep_h.1, bf16[1,2048,2048]{2,1,0:T(8,128)(2,1)} %linv_h.1, bf16[1,2048,2048]{2,1,0:T(8,128)(2,1)} %uinv_h.1, ...), custom_call_target="tpu_custom_call" | custom-call | tf_op jit(solution)/shard_map/supernodal_solve/pallas_call | solution.py:300
  48.0 18.0 %hand_over.1 = (bf16[1,2048,128]{2,1,0:T(8,128)(2,1)}, bf16[128,128]{1,0:T(8,128)(2,1)}) custom-call(bf16[1,2048,128]{2,1,0:T(8,128)(2,1)} %get-tuple-element.4.leaf, bf16[128,128]{1,0:T(8,128)(2,1)} %get-tuple-element.5.sep), custom_call_target="tpu_custom_call" | custom-call | tf_op jit(solution)/shard_map/hand_over/pallas_call | solution.py:324

commit v3 on v2

--- a/solution.py
+++ b/solution.py
@@ -23,11 +23,11 @@
 
 def kernel(
     sizes, offs, rhs_h, rsep_h, linv_h, uinv_h, loff_h, uoff_h, lsep_h, usep_h,
-    out_h, osep_h,
+    out, osep,
     linv, uinv, loff, rhs, mix, gmat, fsol, upd, rsep,
     lcol, urow, macc, mout, mrow,
-    half, recv_half, pieces, rs_in, xs, part, part_in, sol, coupled, obuf, osep,
-    s_rhs, s_linv, s_loff, s_uinv, s_uoff, s_own, s_rsep, s_out, s_osep,
+    half, recv_half, pieces, rs_in, xs, part, part_in, sol, coupled,
+    s_rhs, s_linv, s_loff, s_uinv, s_uoff, s_own, s_rsep,
     l_send, l_recv, u_send, u_recv, uc_sem, m_send, m_recv,
     core_send, core_recv, rs_send, rs_recv, ag_send, ag_recv,
     sem_a,
@@ -100,7 +100,7 @@
         term = dot(loff[:, rows_of(i)], val)
         total[0] = term if total[0] is None else total[0] + term
 
-    for i in range(NT - 2):
+    for i in range(NT - 3):
         front(i)
 
     pl.semaphore_wait(barrier, 19)
@@ -120,7 +120,7 @@
 
         lax.fori_loop(1, 16, body, 0)
 
-    for i in range(NT - 2, NT):
+    for i in range(NT - 3, NT):
         front(i)
     pltpu.make_async_copy(
         uoff_h.at[0], mix.at[:, pl.ds(0, KB * BLK)], s_uoff).start()
@@ -184,6 +184,23 @@
         fsol[rows_of(i), :] = dot(uinv[rows_of(i), span], mix[span, pl.ds(KB * BLK, NR)])
 
     back(0)
+    back(1)
+
+    wait_bytes(rsep, s_rsep)
+    wait_bytes(rs_in.at[pl.ds(0, 63)], rs_recv)
+    gathered = jnp.sum(rs_in[...].astype(F32), axis=0)
+    xs[x * 16 + row] = (rsep[pl.ds(pl.multiple_of(row * 16, 16), 16), :].astype(F32) - gathered).astype(BF)
+
+    def spread(ref, sem):
+        def body(i, carry):
+            pz, py, px = (z + i // 16 + 2) % 4, (y + i // 4 + 2) % 4, (x + i + 2) % 4
+            remote(ref, ref, ag_send.at[sem], ag_recv.at[sem], (pz * 4 + py, px * 2 + k)).start()
+            return carry
+
+        lax.fori_loop(0, 42, body, 0)
+        lax.fori_loop(43, 64, body, 0)
+
+    spread(xs.at[x * 16 + row], 0)
     give_u.wait_recv()
 
     def l_wait(i, carry):
@@ -205,23 +222,6 @@
         px = (x + step) % 4
         remote(mout.at[px], mrow.at[x], m_send, m_recv, along_x(step)).start()
     mrow[x] = mout[x]
-    back(1)
-
-    wait_bytes(rsep, s_rsep)
-    wait_bytes(rs_in.at[pl.ds(0, 63)], rs_recv)
-    gathered = jnp.sum(rs_in[...].astype(F32), axis=0)
-    xs[x * 16 + row] = (rsep[pl.ds(pl.multiple_of(row * 16, 16), 16), :].astype(F32) - gathered).astype(BF)
-
-    def spread(ref, sem):
-        def body(i, carry):
-            pz, py, px = (z + i // 16 + 2) % 4, (y + i // 4 + 2) % 4, (x + i + 2) % 4
-            remote(ref, ref, ag_send.at[sem], ag_recv.at[sem], (pz * 4 + py, px * 2 + k)).start()
-            return carry
-
-        lax.fori_loop(0, 42, body, 0)
-        lax.fori_loop(43, 64, body, 0)
-
-    spread(xs.at[x * 16 + row], 0)
     for i in range(2, 5):
         back(i)
     wait_bytes(mrow.at[pl.ds(0, 3)], m_recv)
@@ -249,18 +249,13 @@
             got = sol[h, named[j]]
             for q in range(4):
                 coupled[pl.ds(BLK * j + 32 * q + 16 * h, 16), :] = got[q]
-    outs = []
     for i in range(NT):
         val = fsol[rows_of(i), :] - dot(gmat[rows_of(i), :], coupled[...])
-        obuf[rows_of(i), :] = jnp.where(keep(TB * i, TB, NR), val, 0.0).astype(BF)
-        outs.append(pltpu.make_async_copy(obuf.at[rows_of(i)], out_h.at[0, rows_of(i)], s_out.at[i]))
-        outs[-1].start()
+        out[0, rows_of(i), :] = jnp.where(keep(TB * i, TB, NR), val, 0.0).astype(BF)
     for h in range(2):
         got = sol[h, row]
         for q in range(4):
             osep[pl.ds(32 * q + 16 * h, 16), :] = got[q]
-    outs.append(pltpu.make_async_copy(osep, osep_h, s_osep))
-    outs[-1].start()
 
     for s in swaps + [swap_m, swap_s, give_u]:
         s.wait_send()
@@ -273,8 +268,6 @@
 
     for sem in (rs_send, ag_send.at[0], ag_send.at[1]):
         wait_bytes(rs_in.at[pl.ds(0, 63)], sem)
-    for o in outs:
-        o.wait()
 
 
 def hand_over(leaf, sep, leaf_out, sep_out, sems):
@@ -293,15 +286,11 @@
     smem = pl.BlockSpec(memory_space=pltpu.SMEM)
     dma = pltpu.SemaphoreType.DMA
     vm = pltpu.VMEM
-    out_shape = (
-        jax.ShapeDtypeStruct((1, W, NR), BF),
-        jax.ShapeDtypeStruct((BLK, NR), BF),
-    )
     solved = pl.pallas_call(
         kernel,
-        out_shape=out_shape,
+        out_shape=(vm((1, W, NR), BF), vm((BLK, NR), BF)),
         in_specs=[smem, smem] + [any_spec] * 8,
-        out_specs=(any_spec, any_spec),
+        out_specs=(pl.BlockSpec(memory_space=vm), pl.BlockSpec(memory_space=vm)),
         scratch_shapes=[
             vm((W, W), BF), vm((W, W), BF), vm((KB * BLK, W), BF), vm((W, NR), BF),
             vm((W, KB * BLK + NR), BF), vm((W, KB * BLK), BF), vm((W, NR), F32),
@@ -311,8 +300,8 @@
             vm((4, 16, 16, NR), BF), vm((4, 16, 16, NR), BF), vm((4, 16, 16, NR), BF),
             vm((64, 16, NR), BF), vm((64, 16, NR), BF),
             vm((2, 16, NR), F32), vm((16, NR), F32), vm((2, 16, 4, 16, NR), BF),
-            vm((KB * BLK, NR), BF), vm((W, NR), BF), vm((BLK, NR), BF),
-            dma((NT,)), dma((NT,)), dma((NT,)), dma((NT,)), dma, dma((2,)), dma, dma((NT,)), dma,
+            vm((KB * BLK, NR), BF),
+            dma((NT,)), dma((NT,)), dma((NT,)), dma((NT,)), dma, dma((2,)), dma,
             dma, dma((16,)), dma, dma, dma((2,)), dma, dma,
             dma((6,)), dma((6,)), dma, dma, dma((2,)), dma((2,)),
             pltpu.SemaphoreType.REGULAR,
@@ -323,11 +312,11 @@
     )(leaf_sizes, off_blocks, rhs_leaf, rhs_sep, linv_leaf, uinv_leaf, l_off, u_off, linv_sep, uinv_sep)
     return pl.pallas_call(
         hand_over,
-        out_shape=out_shape,
-        in_specs=[any_spec, any_spec],
+        out_shape=(jax.ShapeDtypeStruct((1, W, NR), BF), jax.ShapeDtypeStruct((BLK, NR), BF)),
+        in_specs=[pl.BlockSpec(memory_space=vm), pl.BlockSpec(memory_space=vm)],
         out_specs=(any_spec, any_spec),
         scratch_shapes=[dma((2,))],
-        compiler_params=pltpu.CompilerParams(vmem_limit_bytes=56 * 1024 * 1024),
+        compiler_params=pltpu.CompilerParams(vmem_limit_bytes=4 * 1024 * 1024),
         name="hand_over",
     )(*solved)
 

time: 66.2 us -> 47.2 us (0.71)
  Pallas kernels: 64.8 us -> 45.8 us
    pallas_call x2, Pallas kernels: 64.8 us -> 45.8 us  [the longest x1 45 us: shards(): pl.pallas_call(kernel, out_shape=(vm((1, W, NR), BF), vm((BLK, NR), BF)),...]
where the time goes in v3:
time: 47.2 us; the launch traced here: 47.1 us
  Pallas kernels  45.8 us (97%)
  between operations  1.29 us (3%)
    pallas_call x1, Pallas kernels, shards(): pl.pallas_call(kernel, out_shape=(vm((1, W, NR), BF), vm((BLK, NR), BF)),...  45 us

profile of v3, /device:TPU:1, one launch (start us, length us, event | category | flops | bytes accessed | tf_op | source)
XLA Modules:
  0.0 47.1 jit_solution(15005961435010463185)
XLA Ops:
  1.3 45.0 %supernodal_solve.1 = (bf16[1,2048,128]{2,1,0:T(8,128)(2,1)S(1)}, bf16[128,128]{1,0:T(8,128)(2,1)S(1)}) custom-call(s32[1]{0:T(128)S(6)} %copy.12.sizes, s32[1,4]{1,0:T(1,128)} %offs.1, bf16[1,2048,128]{2,1,0:T(8,128)(2,1)} %rhs_h.1, bf16[256,128]{1,0:T(8,128)(2,1)} %rsep_h.1, bf16[1,2048,2048]{2,1,0:T(8,128)(2,1)} %linv_h.1, bf16[1,2048,2048]{2,1,0:T(8,128)(2,1)} %uinv_h.1, ...), custom_call_target="tpu_custom_call" | custom-call | tf_op jit(solution)/shard_map/supernodal_solve/pallas_call | solution.py:289
  46.2 0.8 %hand_over.1 = (bf16[1,2048,128]{2,1,0:T(8,128)(2,1)}, bf16[128,128]{1,0:T(8,128)(2,1)}) custom-call(bf16[1,2048,128]{2,1,0:T(8,128)(2,1)S(1)} %get-tuple-element.4.leaf, bf16[128,128]{1,0:T(8,128)(2,1)S(1)} %get-tuple-element.5.sep), custom_call_target="tpu_custom_call" | custom-call | tf_op jit(solution)/shard_map/hand_over/pallas_call | solution.py:313

commit v4 on v3

--- a/solution.py
+++ b/solution.py
@@ -28,8 +28,8 @@
     lcol, urow, macc, mout, mrow,
     half, recv_half, pieces, rs_in, xs, part, part_in, sol, coupled,
     s_rhs, s_linv, s_loff, s_uinv, s_uoff, s_own, s_rsep,
-    l_send, l_recv, u_send, u_recv, uc_sem, m_send, m_recv,
-    core_send, core_recv, rs_send, rs_recv, ag_send, ag_recv,
+    l_send, l_recv, n_send, n_recv, f_send, f_recv, u_send, u_recv, uc_sem, m_send, m_recv,
+    core_send, core_recv, rs_send, rs_recv, ag_send, ag_recv, sol_recv,
     sem_a,
 ):
     row, col = lax.axis_index("row"), lax.axis_index("col")
@@ -43,6 +43,11 @@
     def along_x(step):
         return (row, ((x + step) % 4) * 2 + k)
 
+    def along(cl, step):
+        if cl == 0:
+            return (z * 4 + (y + step) % 4, col)
+        return (((z + step) % 4) * 4 + y, col)
+
     def wait_bytes(ref, sem):
         pltpu.make_async_copy(ref, ref, sem).wait()
 
@@ -79,7 +84,7 @@
     pl.semaphore_signal(barrier, inc=1, device_id=partner, device_id_type=MESH)
     lax.fori_loop(1, 16, greet, 0)
 
-    pltpu.make_async_copy(lsep_h, lcol.at[row], s_own.at[0]).start()
+    pltpu.make_async_copy(lsep_h, lcol.at[z, y], s_own.at[0]).start()
     pltpu.make_async_copy(usep_h, urow.at[k, x], s_own.at[1]).start()
     pltpu.make_async_copy(rsep_h, rsep, s_rsep).start()
 
@@ -100,28 +105,21 @@
         term = dot(loff[:, rows_of(i)], val)
         total[0] = term if total[0] is None else total[0] + term
 
-    for i in range(NT - 3):
+    for i in range(NT - 1):
         front(i)
 
     pl.semaphore_wait(barrier, 19)
     for step in (1, 2, 3):
         pl.semaphore_signal(sem_a, inc=1, device_id=along_x(step), device_id_type=MESH)
-    wait_bytes(lcol.at[row], s_own.at[0])
+    wait_bytes(lcol.at[z, y], s_own.at[0])
     wait_bytes(urow.at[k, x], s_own.at[1])
     for step in (2, 1, 3):
+        for cl in range(2):
+            ref = lcol.at[z, y, pl.ds(64 * cl, 64)]
+            remote(ref, ref, l_send.at[cl], l_recv.at[cl], along(cl, step)).start()
         remote(urow.at[k, x], urow.at[k, x], u_send, u_recv, along_x(step)).start()
-    filled = row >= 2 * col
-
-    @pl.when(filled)
-    def _():
-        def body(i, carry):
-            remote(lcol.at[row], lcol.at[row], l_send, l_recv.at[row], ((row + i) % 16, col)).start()
-            return carry
-
-        lax.fori_loop(1, 16, body, 0)
-
-    for i in range(NT - 3, NT):
-        front(i)
+
+    front(NT - 1)
     pltpu.make_async_copy(
         uoff_h.at[0], mix.at[:, pl.ds(0, KB * BLK)], s_uoff).start()
     for i in range(NT):
@@ -168,6 +166,21 @@
         else:
             lax.fori_loop(0, 16, rs_body, 0)
 
+    def unit(cl, at, h):
+        if cl == 0:
+            return lcol.at[at, pl.ds(2 * h, 2), pl.ds(0, 64)]
+        return lcol.at[pl.ds(2 * h, 2), at, pl.ds(64, 64)]
+
+    def place(cl, step):
+        return ((z if cl == 0 else y) + step) % 4
+
+    for cl in range(2):
+        wait_bytes(lcol.at[0, pl.ds(0, 3), pl.ds(0, 64)], l_recv.at[cl])
+    for d, h in ((0, 0), (1, 1), (0, 1), (1, 0)):
+        for cl in range(2):
+            ref = unit(cl, place(cl, 0), h)
+            remote(ref, ref, n_send.at[cl, d, h], n_recv.at[cl, d, h], along(1 - cl, 1 + 2 * d)).start()
+
     wait_bytes(urow.at[0, pl.ds(0, 3)], u_recv)
     give_u = remote(urow.at[k], urow.at[k], uc_sem.at[0], uc_sem.at[1], partner)
     give_u.start()
@@ -185,35 +198,37 @@
 
     back(0)
     back(1)
+    for d in range(2):
+        for cl in range(2):
+            ref = unit(cl, place(cl, 3 - 2 * d), d)
+            wait_bytes(ref, n_recv.at[cl, d, d])
+            remote(ref, ref, f_send.at[cl, d], f_recv.at[cl, d], along(1 - cl, 1 + 2 * d)).start()
 
     wait_bytes(rsep, s_rsep)
     wait_bytes(rs_in.at[pl.ds(0, 63)], rs_recv)
     gathered = jnp.sum(rs_in[...].astype(F32), axis=0)
     xs[x * 16 + row] = (rsep[pl.ds(pl.multiple_of(row * 16, 16), 16), :].astype(F32) - gathered).astype(BF)
 
-    def spread(ref, sem):
+    def spread(ref, send, recv):
         def body(i, carry):
             pz, py, px = (z + i // 16 + 2) % 4, (y + i // 4 + 2) % 4, (x + i + 2) % 4
-            remote(ref, ref, ag_send.at[sem], ag_recv.at[sem], (pz * 4 + py, px * 2 + k)).start()
+            remote(ref, ref, send, recv, (pz * 4 + py, px * 2 + k)).start()
             return carry
 
         lax.fori_loop(0, 42, body, 0)
         lax.fori_loop(43, 64, body, 0)
 
-    spread(xs.at[x * 16 + row], 0)
+    spread(xs.at[x * 16 + row], ag_send.at[0], ag_recv)
     give_u.wait_recv()
 
-    def l_wait(i, carry):
-        @pl.when(i != row)
-        def _():
-            wait_bytes(lcol.at[i], l_recv.at[i])
-        return carry
-
-    lax.fori_loop(2 * col, 16, l_wait, 0)
+    for d in range(2):
+        for cl in range(2):
+            wait_bytes(unit(cl, 0, 1 - d), n_recv.at[cl, d, 1 - d])
+            wait_bytes(unit(cl, 0, d), f_recv.at[cl, d])
     macc[...] = jnp.zeros_like(macc)
 
     def m_body(c, carry):
-        macc[...] += dot(urow[c % 2, c // 2], lcol[pl.ds(2 * c, 2)].reshape(TB, TB))
+        macc[...] += dot(urow[c % 2, c // 2], lcol[c // 2, pl.ds(2 * (c % 2), 2)].reshape(TB, TB))
         return carry
 
     lax.fori_loop(jnp.maximum(col, row // 2), 8, m_body, 0)
@@ -225,7 +240,7 @@
     for i in range(2, 5):
         back(i)
     wait_bytes(mrow.at[pl.ds(0, 3)], m_recv)
-    wait_bytes(rs_in.at[pl.ds(0, 63)], ag_recv.at[0])
+    wait_bytes(rs_in.at[pl.ds(0, 63)], ag_recv)
 
     val = None
     for j in range(4):
@@ -236,13 +251,18 @@
     swap_m.start()
     swap_m.wait_recv()
     sol[k, row, x] = (part[k] + part_in[...]).astype(BF)
-    spread(sol.at[k, row, x], 1)
+    spread(sol.at[k, row, x], ag_send.at[1], sol_recv.at[z])
     for i in range(5, NT):
         back(i)
-    wait_bytes(rs_in.at[pl.ds(0, 63)], ag_recv.at[1])
-    swap_s = remote(sol.at[k], sol.at[k], core_send.at[5], core_recv.at[5], partner)
-    swap_s.start()
-    swap_s.wait_recv()
+    last = []
+    for step in (0, 1, 3, 2):
+        pz = (z + step) % 4
+        wait_bytes(rs_in.at[pl.ds(0, 16 if step else 15)], sol_recv.at[pz])
+        ref = sol.at[k, pl.ds(4 * pz, 4)]
+        last.append(remote(ref, ref, core_send.at[5 + step], core_recv.at[5 + step], partner))
+        last[-1].start()
+    for r in last:
+        r.wait_recv()
 
     for j in range(KB):
         for h in range(2):
@@ -257,15 +277,17 @@
         for q in range(4):
             osep[pl.ds(32 * q + 16 * h, 16), :] = got[q]
 
-    for s in swaps + [swap_m, swap_s, give_u]:
+    for s in swaps + last + [swap_m, give_u]:
         s.wait_send()
     wait_bytes(urow.at[0, pl.ds(0, 3)], u_send)
     wait_bytes(mrow.at[pl.ds(0, 3)], m_send)
 
-    @pl.when(filled)
-    def _():
-        wait_bytes(lcol.at[pl.ds(0, 15)], l_send)
-
+    for cl in range(2):
+        wait_bytes(lcol.at[0, pl.ds(0, 3), pl.ds(0, 64)], l_send.at[cl])
+        for d in range(2):
+            wait_bytes(unit(cl, 0, d), f_send.at[cl, d])
+            for h in range(2):
+                wait_bytes(unit(cl, 0, h), n_send.at[cl, d, h])
     for sem in (rs_send, ag_send.at[0], ag_send.at[1]):
         wait_bytes(rs_in.at[pl.ds(0, 63)], sem)
 
@@ -295,15 +317,16 @@
             vm((W, W), BF), vm((W, W), BF), vm((KB * BLK, W), BF), vm((W, NR), BF),
             vm((W, KB * BLK + NR), BF), vm((W, KB * BLK), BF), vm((W, NR), F32),
             vm((KB + 1, 8, 16, NR), BF), vm((TB, NR), BF),
-            vm((16, BLK, TB), BF), vm((2, 4, BLK, TB), BF), vm((BLK, TB), F32),
+            vm((4, 4, BLK, TB), BF), vm((2, 4, BLK, TB), BF), vm((BLK, TB), F32),
             vm((4, 32, TB), BF), vm((4, 32, TB), BF),
             vm((4, 16, 16, NR), BF), vm((4, 16, 16, NR), BF), vm((4, 16, 16, NR), BF),
             vm((64, 16, NR), BF), vm((64, 16, NR), BF),
             vm((2, 16, NR), F32), vm((16, NR), F32), vm((2, 16, 4, 16, NR), BF),
             vm((KB * BLK, NR), BF),
             dma((NT,)), dma((NT,)), dma((NT,)), dma((NT,)), dma, dma((2,)), dma,
-            dma, dma((16,)), dma, dma, dma((2,)), dma, dma,
-            dma((6,)), dma((6,)), dma, dma, dma((2,)), dma((2,)),
+            dma((2,)), dma((2,)), dma((2, 2, 2)), dma((2, 2, 2)), dma((2, 2)), dma((2, 2)),
+            dma, dma, dma((2,)), dma, dma,
+            dma((9,)), dma((9,)), dma, dma, dma((2,)), dma, dma((4,)),
             pltpu.SemaphoreType.REGULAR,
         ],
         compiler_params=pltpu.CompilerParams(

time: 47.2 us -> 44 us (0.932)
  Pallas kernels: 45.8 us -> 42.6 us
    pallas_call x1, Pallas kernels: 45 us -> 41.8 us  [shards(): pl.pallas_call(kernel, out_shape=(vm((1, W, NR), BF), vm((BLK, NR), BF)),...]
where the time goes in v4:
time: 44 us; the launch traced here: 43.9 us
  Pallas kernels  42.6 us (97%)
  between operations  1.29 us (3%)
    pallas_call x1, Pallas kernels, shards(): pl.pallas_call(kernel, out_shape=(vm((1, W, NR), BF), vm((BLK, NR), BF)),...  41.8 us

profile of v4, /device:TPU:1, one launch (start us, length us, event | category | flops | bytes accessed | tf_op | source)
XLA Modules:
  0.0 43.9 jit_solution(10685319349105478918)
XLA Ops:
  1.3 41.8 %supernodal_solve.1 = (bf16[1,2048,128]{2,1,0:T(8,128)(2,1)S(1)}, bf16[128,128]{1,0:T(8,128)(2,1)S(1)}) custom-call(s32[1]{0:T(128)S(6)} %copy.12.sizes, s32[1,4]{1,0:T(1,128)} %offs.1, bf16[1,2048,128]{2,1,0:T(8,128)(2,1)} %rhs_h.1, bf16[256,128]{1,0:T(8,128)(2,1)} %rsep_h.1, bf16[1,2048,2048]{2,1,0:T(8,128)(2,1)} %linv_h.1, bf16[1,2048,2048]{2,1,0:T(8,128)(2,1)} %uinv_h.1, ...), custom_call_target="tpu_custom_call" | custom-call | tf_op jit(solution)/shard_map/supernodal_solve/pallas_call | solution.py:311
  43.1 0.8 %hand_over.1 = (bf16[1,2048,128]{2,1,0:T(8,128)(2,1)}, bf16[128,128]{1,0:T(8,128)(2,1)}) custom-call(bf16[1,2048,128]{2,1,0:T(8,128)(2,1)S(1)} %get-tuple-element.4.leaf, bf16[128,128]{1,0:T(8,128)(2,1)S(1)} %get-tuple-element.5.sep), custom_call_target="tpu_custom_call" | custom-call | tf_op jit(solution)/shard_map/hand_over/pallas_call | solution.py:336

commit v5 on v4

v5 whole, which is shorter than its diff:
```python
import jax
import jax.numpy as jnp
from jax import lax
from jax.experimental import pallas as pl
from jax.experimental.pallas import tpu as pltpu
from jax.sharding import PartitionSpec as P

MESH = pl.DeviceIdType.MESH
W = 2048
NR = 128
BLK = 128
KB = 4
TB = 256
NT = W // TB
WINDOW = 4
EARLY = 4
FAR_PLANE = sorted(
    [(i // 4, i % 4) for i in range(1, 16)],
    key=lambda d: -(min(d[0], 4 - d[0]) + min(d[1], 4 - d[1])))
BF = jnp.bfloat16
F32 = jnp.float32


def dot(a, b):
    return jnp.dot(a, b, preferred_element_type=F32)


def kernel(
    sizes_h, offs_h, rhs_h, rsep_h, linv_h, uinv_h, loff_h, uoff_h, lsep_h, usep_h,
    gmat, fsol, coupled, osep,
    linv, uinv, loff, rhs, mix, upd, rsep,
    lcol, urow, macc,
    half, recv_half, pieces, rs_in, xs, part, part_in, sol,
    s_front, s_back, s_own, s_send, l_recv, u_recv, near_recv, m_recv, p_recv,
    swap_recv, last_recv, rs_recv, ag_recv, sol_recv,
    sem_a, sizes, offs, s_sizes, s_offs,
):
    row, col = lax.axis_index("row"), lax.axis_index("col")
    z, y = row // 4, row % 4
    x, k = col // 2, col % 2
    other = 1 - k
    chip = z * 16 + y * 4 + x
    partner = (row, x * 2 + other)

    def along_x(step):
        return (row, ((x + step) % 4) * 2 + k)

    def along(cl, step):
        if cl == 0:
            return (z * 4 + (y + step) % 4, col)
        return (((z + step) % 4) * 4 + y, col)

    def wait_bytes(ref, sem):
        pltpu.make_async_copy(ref, ref, sem).wait()

    def wait_kib(count, sem):
        wait_bytes(linv.at[pl.ds(0, count // 4)], sem)

    def remote(src, dst, recv, device):
        return pltpu.make_async_remote_copy(
            src_ref=src, dst_ref=dst, send_sem=s_send, recv_sem=recv,
            device_id=device, device_id_type=MESH)

    def keep(start, rows, cols):
        return lax.broadcasted_iota(jnp.int32, (rows, cols), 0) + start < sizes[0]

    def rows_of(i):
        return pl.ds(TB * i, TB)

    def load_front(i):
        pltpu.make_async_copy(rhs_h.at[0, rows_of(i)], rhs.at[rows_of(i)], s_front.at[i % WINDOW]).start()
        span = pl.ds(0, TB * (i + 1))
        pltpu.make_async_copy(
            linv_h.at[0, rows_of(i), span], linv.at[rows_of(i), span], s_front.at[i % WINDOW]).start()
        pltpu.make_async_copy(
            loff_h.at[0, :, rows_of(i)], loff.at[:, rows_of(i)], s_front.at[i % WINDOW]).start()

    pltpu.make_async_copy(sizes_h, sizes, s_sizes).start()
    for i in range(WINDOW):
        load_front(i)
    pltpu.make_async_copy(offs_h, offs, s_offs).start()

    barrier = pltpu.get_barrier_semaphore()

    def greet(i, carry):
        pl.semaphore_signal(barrier, inc=1, device_id=((row + i) % 16, col), device_id_type=MESH)
        return carry

    for step in range(1, 8):
        pl.semaphore_signal(barrier, inc=1, device_id=(row, (col + step) % 8), device_id_type=MESH)
    lax.fori_loop(1, 16, greet, 0)

    pltpu.make_async_copy(lsep_h, lcol.at[z, y], s_own).start()
    pltpu.make_async_copy(usep_h, urow.at[k, x], s_own).start()
    pltpu.make_async_copy(rsep_h, rsep, s_own).start()

    def factors():
        pl.semaphore_wait(barrier, 22)
        for step in range(1, 8):
            pl.semaphore_signal(sem_a, inc=1, device_id=(row, (col + step) % 8), device_id_type=MESH)
        wait_kib(192, s_own)
        for step in (2, 1, 3):
            for cl in range(2):
                ref = lcol.at[z, y, pl.ds(64 * cl, 64)]
                remote(ref, ref, l_recv, along(cl, step)).start()
            remote(urow.at[k, x], urow.at[k, x], u_recv, along_x(step)).start()

    total = None
    before = None
    wait_bytes(sizes, s_sizes)
    for i in range(NT):
        span = pl.ds(0, TB * (i + 1))
        wait_kib(64 * (2 * i + 7), s_front.at[i % WINDOW])
        if i + WINDOW < NT:
            load_front(i + WINDOW)
        mask = keep(TB * i, TB, NR)
        rhs[rows_of(i), :] = jnp.where(mask, rhs[rows_of(i), :].astype(F32), 0.0).astype(BF)
        val = dot(linv[rows_of(i), span], rhs[span, :])
        val = jnp.where(mask, val, 0.0).astype(BF)
        mix[rows_of(i), pl.ds(KB * BLK, NR)] = val
        if before is not None:
            term = dot(loff[:, rows_of(i - 1)], before)
            total = term if total is None else total + term
        before = val
        if i == EARLY:
            factors()

    total = total + dot(loff[:, rows_of(NT - 1)], before)
    pltpu.make_async_copy(
        uoff_h.at[0], mix.at[:, pl.ds(0, KB * BLK)], s_back).start()
    for i in range(NT):
        span = pl.ds(TB * i, W - TB * i)
        pltpu.make_async_copy(
            uinv_h.at[0, rows_of(i), span], uinv.at[rows_of(i), span], s_back).start()

    for j in range(KB):
        upd[j] = total[BLK * j:BLK * (j + 1), :].reshape(8, 16, NR).astype(BF)
    upd[KB] = jnp.zeros((8, 16, NR), BF)
    wait_bytes(offs, s_offs)
    named = [offs[0, j] for j in range(KB)]

    def block(s):
        at = jnp.int32(KB)
        for j in range(KB):
            at = jnp.where(named[j] == s, j, at)
        return upd[at]

    swaps = []
    for j in range(4):
        c4 = (x + 2 + j) % 4
        for b in range(2):
            half[j, pl.ds(8 * b, 8)] = block(4 * c4 + 2 * other + b)
        swaps.append(remote(half.at[j], recv_half.at[j], swap_recv.at[j], partner))
        swaps[-1].start()
    pl.semaphore_wait(sem_a, 7)
    for j in range(4):
        c4 = (x + 2 + j) % 4
        swaps[j].wait_recv()
        for b in range(2):
            mine = block(4 * c4 + 2 * k + b).astype(F32)
            got = recv_half[j, pl.ds(8 * b, 8)].astype(F32)
            pieces[c4, pl.ds(8 * b, 8)] = (mine + got).astype(BF)

        def rs_body(i, carry, c4=c4):
            prow = ((z + i // 4 + 2) % 4) * 4 + (y + i + 2) % 4
            remote(pieces.at[c4, prow], rs_in.at[chip], rs_recv, (prow, c4 * 2 + k)).start()
            return carry

        if j == 2:
            lax.fori_loop(0, 10, rs_body, 0)
            lax.fori_loop(11, 16, rs_body, 0)
            rs_in[chip] = pieces[c4, row]
        else:
            lax.fori_loop(0, 16, rs_body, 0)

    def unit(cl, at, h):
        if cl == 0:
            return lcol.at[at, pl.ds(2 * h, 2), pl.ds(0, 64)]
        return lcol.at[pl.ds(2 * h, 2), at, pl.ds(64, 64)]

    def place(cl, step):
        return ((z if cl == 0 else y) + step) % 4

    wait_kib(192, l_recv)
    for d, h in ((0, 0), (1, 1), (0, 1), (1, 0)):
        for cl in range(2):
            ref = unit(cl, place(cl, 0), h)
            remote(ref, ref, near_recv if d == h else m_recv, along(1 - cl, 1 + 2 * d)).start()

    wait_kib(192, u_recv)
    remote(urow.at[k], urow.at[k], m_recv, partner).start()

    wait_kib(36 * 128 + 2048, s_back)
    for i in range(NT):
        val = mix[rows_of(i), pl.ds(0, KB * BLK)].astype(F32)
        mix[rows_of(i), pl.ds(0, KB * BLK)] = jnp.where(keep(TB * i, TB, KB * BLK), val, 0.0).astype(BF)

    def back(i):
        span = pl.ds(TB * i, W - TB * i)
        val = dot(uinv[rows_of(i), span], mix[span, pl.ds(0, KB * BLK)])
        gmat[rows_of(i), :] = jnp.where(keep(TB * i, TB, KB * BLK), val, 0.0).astype(BF)
        val = dot(uinv[rows_of(i), span], mix[span, pl.ds(KB * BLK, NR)])
        fsol[rows_of(i), :] = jnp.where(keep(TB * i, TB, NR), val, 0.0)

    back(0)
    back(1)
    wait_kib(256, near_recv)
    for d in range(2):
        for cl in range(2):
            ref = unit(cl, place(cl, 3 - 2 * d), d)
            remote(ref, ref, m_recv, along(1 - cl, 1 + 2 * d)).start()

    wait_bytes(rs_in.at[pl.ds(0, 63)], rs_recv)
    gathered = jnp.sum(rs_in[...].astype(F32), axis=0)
    xs[row] = (rsep[pl.ds(pl.multiple_of(row * 16, 16), 16), :].astype(F32) - gathered).astype(BF)

    for dz, dy in FAR_PLANE:
        remote(xs.at[row], xs.at[row], ag_recv, (((z + dz) % 4) * 4 + (y + dy) % 4, col)).start()
    for i in range(2, 5):
        back(i)

    wait_kib(768, m_recv)
    macc[...] = jnp.zeros_like(macc)

    def m_body(c, carry):
        macc[...] += dot(urow[c % 2, c // 2], lcol[c // 2, pl.ds(2 * (c % 2), 2)].reshape(TB, TB))
        return carry

    lax.fori_loop(jnp.maximum(col, row // 2), 8, m_body, 0)
    factor = macc[...].astype(BF)
    wait_bytes(xs.at[pl.ds(0, 15)], ag_recv)
    part[...] = dot(factor, xs[...].reshape(TB, NR)).reshape(8, 16, NR)

    for step in (4, 5, 3, 2, 6, 7, 1):
        to = (col + step) % 8
        remote(part.at[to], part_in.at[col], p_recv, (row, to)).start()
    part_in[col] = part[col]
    wait_bytes(part.at[pl.ds(0, 7)], p_recv)
    sol[k, row, x] = jnp.sum(part_in[...], axis=0).astype(BF)

    mine = sol.at[k, row, x]

    def sol_body(i, carry):
        pz, py, px = (z + i // 16 + 2) % 4, (y + i // 4 + 2) % 4, (x + i + 2) % 4
        remote(mine, mine, sol_recv.at[z], (pz * 4 + py, px * 2 + k)).start()
        return carry

    lax.fori_loop(0, 42, sol_body, 0)
    lax.fori_loop(43, 64, sol_body, 0)
    for i in range(5, NT):
        back(i)
    for step in (0, 1, 3, 2):
        pz = (z + step) % 4
        wait_bytes(rs_in.at[pl.ds(0, 16 if step else 15)], sol_recv.at[pz])
        ref = sol.at[k, pl.ds(4 * pz, 4)]
        remote(ref, ref, last_recv, partner).start()
    wait_kib(256, last_recv)

    for j in range(KB):
        for h in range(2):
            got = sol[h, named[j]]
            for q in range(4):
                coupled[pl.ds(BLK * j + 32 * q + 16 * h, 16), :] = got[q]
    for h in range(2):
        got = sol[h, row]
        for q in range(4):
            osep[pl.ds(32 * q + 16 * h, 16), :] = got[q]

    wait_kib(2496, s_send)
    wait_bytes(fsol.at[pl.ds(0, 88)], s_send)


def finish(gmat, fsol, coupled, sep, leaf_out, sep_out, leaf, sems):
    copies = [pltpu.make_async_copy(sep, sep_out, sems.at[0])]
    copies[0].start()
    for i in range(0, NT, 2):
        rows = pl.ds(TB * i, 2 * TB)
        leaf[rows, :] = (fsol[rows, :] - dot(gmat[rows, :], coupled[...])).astype(BF)
        copies.append(pltpu.make_async_copy(leaf.at[rows], leaf_out.at[0, rows], sems.at[1 + i // 2]))
        copies[-1].start()
    for copy in copies:
        copy.wait()


def shards(
    rhs_leaf, rhs_sep, leaf_sizes, off_blocks, linv_leaf, uinv_leaf, l_off, u_off, linv_sep, uinv_sep,
):
    any_spec = pl.BlockSpec(memory_space=pl.ANY)
    dma = pltpu.SemaphoreType.DMA
    vm = pltpu.VMEM
    solved = pl.pallas_call(
        kernel,
        out_shape=(vm((W, KB * BLK), BF), vm((W, NR), F32), vm((KB * BLK, NR), BF), vm((BLK, NR), BF)),
        in_specs=[any_spec] * 10,
        out_specs=(pl.BlockSpec(memory_space=vm),) * 4,
        scratch_shapes=[
            vm((W, W), BF), vm((W, W), BF), vm((KB * BLK, W), BF), vm((W, NR), BF),
            vm((W, KB * BLK + NR), BF),
            vm((KB + 1, 8, 16, NR), BF), vm((TB, NR), BF),
            vm((4, 4, BLK, TB), BF), vm((2, 4, BLK, TB), BF), vm((BLK, TB), F32),
            vm((4, 16, 16, NR), BF), vm((4, 16, 16, NR), BF), vm((4, 16, 16, NR), BF),
            vm((64, 16, NR), BF), vm((16, 16, NR), BF),
            vm((8, 16, NR), F32), vm((8, 16, NR), F32), vm((2, 16, 4, 16, NR), BF),
            dma((WINDOW,)), dma, dma, dma, dma, dma, dma, dma, dma,
            dma((4,)), dma, dma, dma, dma((4,)),
            pltpu.SemaphoreType.REGULAR, pltpu.SMEM((1,), jnp.int32), pltpu.SMEM((1, KB), jnp.int32), dma, dma,
        ],
        compiler_params=pltpu.CompilerParams(
            collective_id=0, has_side_effects=True, vmem_limit_bytes=56 * 1024 * 1024),
        name="supernodal_solve",
    )(leaf_sizes, off_blocks, rhs_leaf, rhs_sep, linv_leaf, uinv_leaf, l_off, u_off, linv_sep, uinv_sep)
    return pl.pallas_call(
        finish,
        out_shape=(jax.ShapeDtypeStruct((1, W, NR), BF), jax.ShapeDtypeStruct((BLK, NR), BF)),
        in_specs=[pl.BlockSpec(memory_space=vm)] * 4,
        out_specs=(any_spec, any_spec),
        scratch_shapes=[vm((W, NR), BF), dma((1 + NT // 2,))],
        compiler_params=pltpu.CompilerParams(vmem_limit_bytes=8 * 1024 * 1024),
        name="leaf_finish",
    )(*solved)


def solution(mesh):
    placed = (
        P(("row", "col"), None, None),
        P("col", None),
        P(("row", "col")),
        P(("row", "col"), None),
        P(("row", "col"), None, None),
        P(("row", "col"), None, None),
        P(("row", "col"), None, None),
        P(("row", "col"), None, None),
        P("row", "col"),
        P("row", "col"),
    )
    return jax.shard_map(
        shards,
        mesh=mesh,
        in_specs=placed,
        out_specs=(P(("row", "col"), None, None), P("row", None)),
        check_vma=False,
    )
```

time: 44 us -> 40.3 us (0.916)
  Pallas kernels: 42.6 us -> 38.9 us
    pallas_call x2, Pallas kernels: 42.6 us -> 38.9 us  [the longest x1 37.4 us: shards(): pl.pallas_call(kernel, out_shape=(vm((W, KB * BLK), BF), vm((W, NR), F32)...]
where the time goes in v5:
time: 40.3 us; the launch traced here: 40.2 us
  Pallas kernels  38.9 us (97%)
  between operations  1.29 us (3%)
    pallas_call x1, Pallas kernels, shards(): pl.pallas_call(kernel, out_shape=(vm((W, KB * BLK), BF), vm((W, NR), F32)...  37.4 us
    pallas_call x1, Pallas kernels, shards(): pl.pallas_call(finish, out_shape=(jax.ShapeDtypeStruct((1, W, NR), BF), j...  1.46 us

profile of v5, /device:TPU:1, one launch (start us, length us, event | category | flops | bytes accessed | tf_op | source)
XLA Modules:
  0.0 40.2 jit_solution(11976766675643965664)
XLA Ops:
  1.3 37.4 %supernodal_solve.1 = (bf16[2048,512]{1,0:T(8,128)(2,1)S(1)}, f32[2048,128]{1,0:T(8,128)S(1)}, bf16[512,128]{1,0:T(8,128)(2,1)S(1)}, bf16[128,128]{1,0:T(8,128)(2,1)S(1)}) custom-call(s32[1]{0:T(128)S(6)} %copy.12.sizes_h, s32[1,4]{1,0:T(1,128)} %offs_h.1, bf16[1,2048,128]{2,1,0:T(8,128)(2,1)} %rhs_h.1, bf16[256,128]{1,0:T(8,128)(2,1)} %rsep_h.1, ...), custom_call_target="tpu_custom_call" | custom-call | tf_op jit(solution)/shard_map/supernodal_solve/pallas_call | solution.py:291
  38.7 1.5 %leaf_finish.1 = (bf16[1,2048,128]{2,1,0:T(8,128)(2,1)}, bf16[128,128]{1,0:T(8,128)(2,1)}) custom-call(bf16[2048,512]{1,0:T(8,128)(2,1)S(1)} %get-tuple-element.6.gmat, f32[2048,128]{1,0:T(8,128)S(1)} %get-tuple-element.7.fsol, bf16[512,128]{1,0:T(8,128)(2,1)S(1)} %get-tuple-element.8.coupled, bf16[128,128]{1,0:T(8,128)(2,1)S(1)} %get-tuple-element.9.sep), custom_call_target="tpu_custom_call" | custom-call | tf_op jit(solution)/shard_map/leaf_finish/pallas_call | solution.py:312

commit v6 on v5

--- a/solution.py
+++ b/solution.py
@@ -204,18 +204,17 @@
 
     back(0)
     back(1)
+    wait_bytes(rs_in.at[pl.ds(0, 63)], rs_recv)
+    gathered = jnp.sum(rs_in[...].astype(F32), axis=0)
+    xs[row] = (rsep[pl.ds(pl.multiple_of(row * 16, 16), 16), :].astype(F32) - gathered).astype(BF)
+
+    for dz, dy in FAR_PLANE:
+        remote(xs.at[row], xs.at[row], ag_recv, (((z + dz) % 4) * 4 + (y + dy) % 4, col)).start()
     wait_kib(256, near_recv)
     for d in range(2):
         for cl in range(2):
             ref = unit(cl, place(cl, 3 - 2 * d), d)
             remote(ref, ref, m_recv, along(1 - cl, 1 + 2 * d)).start()
-
-    wait_bytes(rs_in.at[pl.ds(0, 63)], rs_recv)
-    gathered = jnp.sum(rs_in[...].astype(F32), axis=0)
-    xs[row] = (rsep[pl.ds(pl.multiple_of(row * 16, 16), 16), :].astype(F32) - gathered).astype(BF)
-
-    for dz, dy in FAR_PLANE:
-        remote(xs.at[row], xs.at[row], ag_recv, (((z + dz) % 4) * 4 + (y + dy) % 4, col)).start()
     for i in range(2, 5):
         back(i)
 

time: 40.3 us -> 39.9 us (0.990)
    pallas_call x1, Pallas kernels: 37.4 us -> 37 us  [shards(): pl.pallas_call(kernel, out_shape=(vm((W, KB * BLK), BF), vm((W, NR), F32)...]
where the time goes in v6:
time: 39.9 us; the launch traced here: 39.7 us
  Pallas kernels  38.5 us (96%)
  between operations  1.29 us (3%)
    pallas_call x1, Pallas kernels, shards(): pl.pallas_call(kernel, out_shape=(vm((W, KB * BLK), BF), vm((W, NR), F32)...  37 us
    pallas_call x1, Pallas kernels, shards(): pl.pallas_call(finish, out_shape=(jax.ShapeDtypeStruct((1, W, NR), BF), j...  1.46 us

profile of v6, /device:TPU:1, one launch (start us, length us, event | category | flops | bytes accessed | tf_op | source)
XLA Modules:
  0.0 39.7 jit_solution(8293835482941820660)
XLA Ops:
  1.3 37.0 %supernodal_solve.1 = (bf16[2048,512]{1,0:T(8,128)(2,1)S(1)}, f32[2048,128]{1,0:T(8,128)S(1)}, bf16[512,128]{1,0:T(8,128)(2,1)S(1)}, bf16[128,128]{1,0:T(8,128)(2,1)S(1)}) custom-call(s32[1]{0:T(128)S(6)} %copy.12.sizes_h, s32[1,4]{1,0:T(1,128)} %offs_h.1, bf16[1,2048,128]{2,1,0:T(8,128)(2,1)} %rhs_h.1, bf16[256,128]{1,0:T(8,128)(2,1)} %rsep_h.1, ...), custom_call_target="tpu_custom_call" | custom-call | tf_op jit(solution)/shard_map/supernodal_solve/pallas_call | solution.py:290
  38.3 1.5 %leaf_finish.1 = (bf16[1,2048,128]{2,1,0:T(8,128)(2,1)}, bf16[128,128]{1,0:T(8,128)(2,1)}) custom-call(bf16[2048,512]{1,0:T(8,128)(2,1)S(1)} %get-tuple-element.6.gmat, f32[2048,128]{1,0:T(8,128)S(1)} %get-tuple-element.7.fsol, bf16[512,128]{1,0:T(8,128)(2,1)S(1)} %get-tuple-element.8.coupled, bf16[128,128]{1,0:T(8,128)(2,1)S(1)} %get-tuple-element.9.sep), custom_call_target="tpu_custom_call" | custom-call | tf_op jit(solution)/shard_map/leaf_finish/pallas_call | solution.py:311

commit v7 on v6

--- a/solution.py
+++ b/solution.py
@@ -13,7 +13,7 @@
 TB = 256
 NT = W // TB
 WINDOW = 4
-EARLY = 4
+EARLY = 3
 FAR_PLANE = sorted(
     [(i // 4, i % 4) for i in range(1, 16)],
     key=lambda d: -(min(d[0], 4 - d[0]) + min(d[1], 4 - d[1])))

time: 39.9 us -> 39.8 us (level)
  no operation moved by 1% of the time
where the time goes in v7:
time: 39.8 us; the launch traced here: 39.7 us
  Pallas kernels  38.4 us (96%)
  between operations  1.29 us (3%)
    pallas_call x1, Pallas kernels, shards(): pl.pallas_call(kernel, out_shape=(vm((W, KB * BLK), BF), vm((W, NR), F32)...  36.9 us
    pallas_call x1, Pallas kernels, shards(): pl.pallas_call(finish, out_shape=(jax.ShapeDtypeStruct((1, W, NR), BF), j...  1.46 us

profile of v7, /device:TPU:1, one launch (start us, length us, event | category | flops | bytes accessed | tf_op | source)
XLA Modules:
  0.0 39.7 jit_solution(3141440999174846675)
XLA Ops:
  1.3 36.9 %supernodal_solve.1 = (bf16[2048,512]{1,0:T(8,128)(2,1)S(1)}, f32[2048,128]{1,0:T(8,128)S(1)}, bf16[512,128]{1,0:T(8,128)(2,1)S(1)}, bf16[128,128]{1,0:T(8,128)(2,1)S(1)}) custom-call(s32[1]{0:T(128)S(6)} %copy.12.sizes_h, s32[1,4]{1,0:T(1,128)} %offs_h.1, bf16[1,2048,128]{2,1,0:T(8,128)(2,1)} %rhs_h.1, bf16[256,128]{1,0:T(8,128)(2,1)} %rsep_h.1, ...), custom_call_target="tpu_custom_call" | custom-call | tf_op jit(solution)/shard_map/supernodal_solve/pallas_call | solution.py:290
  38.2 1.5 %leaf_finish.1 = (bf16[1,2048,128]{2,1,0:T(8,128)(2,1)}, bf16[128,128]{1,0:T(8,128)(2,1)}) custom-call(bf16[2048,512]{1,0:T(8,128)(2,1)S(1)} %get-tuple-element.6.gmat, f32[2048,128]{1,0:T(8,128)S(1)} %get-tuple-element.7.fsol, bf16[512,128]{1,0:T(8,128)(2,1)S(1)} %get-tuple-element.8.coupled, bf16[128,128]{1,0:T(8,128)(2,1)S(1)} %get-tuple-element.9.sep), custom_call_target="tpu_custom_call" | custom-call | tf_op jit(solution)/shard_map/leaf_finish/pallas_call | solution.py:311
